TPU v7x, 768 devices: a whole 4x8x12 slice. The times are simulated.
768 devices in a mesh: grid: 24 (over y_lo, z), band: 32 (over x, y_hi, core).
Axes of the slice: x: 4, y: 8 (y_hi: 4, y_lo: 2; y = y_hi * 2 + y_lo), z: 12, core: 2. Of those that a mesh axis runs over, the one named last changes fastest.
Arguments:
- psi_block: float32 [8, 96, 32, 128], P(None, 'grid'), may hold values from -6 to 6
- occupied: float32 [32, 96, 32, 128], P('band', 'grid'), may hold values from -6 to 6
- entry_cell: int32 [24576], P('grid'), may hold values from 0 to 16383
- entry_proj: int32 [24576], P('grid'), may hold values from 0 to 767
- entry_value: float32 [24576], P('grid'), may hold values from -3 to 3
- proj_gain: float32 [768], replicated, may hold values from 0.3 to 3
Outputs:
- applied: float32 [8, 96, 32, 128], P(None, 'grid')
All inputs are finite; a program needn't handle non-finite values.
Results may differ from a plain program's by a relative error of at most 0.00002.
Values sent between devices are 32-bit elements; how exact they have to be, the bound alone decides.
A program may use at most 64 MiB of HBM per device.

v0:
```python
import jax
import jax.numpy as jnp
from jax import lax
from jax.sharding import PartitionSpec as P

SWEEPS = 4


screening = 0.5
mixing = 0.25


def extended(x, sides, width):
    for axis, dim in sides:
        size, length = (lax.axis_size(axis), x.shape[dim])
        up = [(i, (i + 1) % size) for i in range(size)]
        down = [(j, i) for i, j in up]
        last = lax.slice_in_dim(x, length - width, length, axis=dim)
        initial = lax.slice_in_dim(x, 0, width, axis=dim)
        before = lax.ppermute(last, axis, up)
        after = lax.ppermute(initial, axis, down)
        x = jnp.concatenate([before, x, after], axis=dim)
    return x


def relax_once(padded, density):
    center = padded[:, 1:-1]
    summed = padded[:, 2:] + padded[:, :-2]
    summed = summed + jnp.roll(center, -1, 2) + jnp.roll(center, 1, 2)
    summed = summed + jnp.roll(center, -1, 3) + jnp.roll(center, 1, 3)
    return (summed + density) / (6.0 + screening)


def per_device(psi_block, occupied, entry_cell, entry_proj, entry_value, proj_gain):
    nblock = psi_block.shape[0]
    nocc = occupied.shape[0]
    planes = psi_block.shape[1]
    rest = psi_block.shape[2:]
    flattened = psi_block.reshape(nblock, -1)
    values = flattened[:, entry_cell]
    coefficient = jax.ops.segment_sum(
        (values * entry_value[None, :]).T, entry_proj, num_segments=proj_gain.shape[0]
    )
    coefficient = lax.psum(coefficient, "grid")
    scaled = coefficient * proj_gain[:, None]
    contrib = entry_value[:, None] * scaled[entry_proj]
    nonlocal_term = jax.ops.segment_sum(
        contrib, entry_cell, num_segments=flattened.shape[1]
    ).T.reshape(psi_block.shape)
    block_padded = extended(psi_block, (("grid", 1),), 1)
    density = (psi_block[:, None] * occupied[None]).reshape((nblock * nocc, planes) + rest)
    potential = density / (6.0 + screening)
    for sweep_index in range(SWEEPS - 1):
        padded = extended(potential, (("grid", 1),), 1)
        potential = relax_once(padded, density)
    neighbour_sum = relax_once(block_padded, jnp.zeros_like(psi_block)) * (6.0 + screening)
    kinetic = -0.5 * (neighbour_sum - 6.0 * psi_block)
    potential = potential.reshape((nblock, nocc, planes) + rest)
    partial_value = jnp.sum(occupied[None] * potential, axis=1)
    summed = lax.psum(partial_value, "band")
    exchange = -mixing * summed
    return kinetic + nonlocal_term + exchange


def solution(mesh):
    in_specs = (
        P(None, "grid", None, None),
        P("band", "grid", None, None),
        P("grid"),
        P("grid"),
        P("grid"),
        P(),
    )
    out_specs = P(None, "grid", None, None)
    return jax.shard_map(
        per_device, mesh=mesh, in_specs=in_specs, out_specs=out_specs, check_vma=False
    )
```

profile of v0, /device:TPU:1, one launch (start us, length us, event | category | flops | bytes accessed | tf_op | source)
XLA Modules:
  0.0 481.2 jit_solution(9032115912352326759)
XLA Ops:
  6.5 1.7 fusion.61
  8.3 4.8 %collective-permute-start.1 = (f32[8,1,32,128]{3,2,1,0:T(8,128)}, f32[8,1,32,128]{3,2,1,0:T(8,128)S(1)}, u32[]{:S(2)}, u32[]{:S(2)}) collective-permute-start(f32[8,1,32,128]{3,2,1,0:T(8,128)} %get-tuple-element.44), channel_id=1, source_target_pairs={{0,32},{32,64},{64,96},{96,128},{128,160},{160,192},{192,224},{224... | collective-permute-start | bytes 393224 | tf_op jit(solution)/shard_map/ppermute | solution.py:20
  13.1 13.2 %collective-permute-start = (f32[8,1,32,128]{3,2,1,0:T(8,128)}, f32[8,1,32,128]{3,2,1,0:T(8,128)S(1)}, u32[]{:S(2)}, u32[]{:S(2)}) collective-permute-start(f32[8,1,32,128]{3,2,1,0:T(8,128)} %get-tuple-element.43), channel_id=1, source_target_pairs={{32,0},{64,32},{96,64},{128,96},{160,128},{192,160},{224,192},{256... | collective-permute-start | bytes 393224 | tf_op jit(solution)/shard_map/ppermute | solution.py:21
  26.3 1.1 multiply_multiply_fusion
  27.5 0.7 fusion.56
  28.2 1.9 collective-permute-start.3
  30.1 5.6 %collective-permute-start.2 = (f32[8,1,32,128]{3,2,1,0:T(8,128)}, f32[8,1,32,128]{3,2,1,0:T(8,128)}, u32[]{:S(2)}, u32[]{:S(2)}) collective-permute-start(f32[8,1,32,128]{3,2,1,0:T(8,128)} %get-tuple-element.33), channel_id=1, source_target_pairs={{32,0},{64,32},{96,64},{128,96},{160,128},{192,160},{224,192},{256... | collective-permute-start | bytes 393224 | tf_op jit(solution)/shard_map/ppermute | solution.py:21
  35.7 5.9 %copy.8 = f32[8,4,32,128]{0,3,2,1:T(8,128)} copy(f32[8,4,32,128]{3,2,1,0:T(8,128)} %param.6) | data formatting | bytes 1048576 | tf_op args[0]
  41.7 1.1 fusion.60
  42.8 1.1 fusion.57
  44.0 0.2 fusion.52
  44.3 1.2 fusion.53
  45.4 13.0 %scatter_custom_fusion = f32[768,8]{1,0:T(8,128)} fusion(s32[1024]{0:T(1024)S(1)} %copy-done.9, f32[1024]{0:T(1024)S(1)} %copy-done.7, f32[]{:T(128)} %constant.6.clone.1, f32[8,16384]{0,1:T(8,128)} %bitcast.6, s32[1024]{0:T(1024)S(1)} %fusion.38), kind=kCustom, calls=%fused_computation.44 | custom fusion | flops 16384 | bytes 557060 | tf_op jit(solution)/shard_map/scatter-add | solution.py:41
  58.5 72.6 %psum.14 = f32[768,8]{1,0:T(8,128)} all-reduce(f32[768,8]{1,0:T(8,128)} %scatter_custom_fusion), channel_id=1, replica_groups=mesh['grid'=24,'band'=32] {'grid'}, use_global_device_ids=true, to_apply=%region_1.0 | all-reduce | flops 6144 | bytes 49152 | tf_op jit(solution)/shard_map/psum | solution.py:44
  131.1 1.9 broadcast_multiply_fusion
  133.0 1.9 fusion.22
  135.3 0.2 fusion.48
  135.5 2.1 collective-permute-start.5
  137.6 5.3 %collective-permute-start.4 = (f32[8,1,32,128]{3,2,1,0:T(8,128)S(1)}, f32[8,1,32,128]{3,2,1,0:T(8,128)S(1)}, u32[]{:S(2)}, u32[]{:S(2)}) collective-permute-start(f32[8,1,32,128]{3,2,1,0:T(8,128)S(1)} %get-tuple-element.23), channel_id=1, source_target_pairs={{32,0},{64,32},{96,64},{128,96},{160,128},{192,160},{224,192},{256... | collective-permute-start | bytes 393224 | tf_op jit(solution)/shard_map/ppermute | solution.py:21
  143.0 0.4 collective-permute-done.5
  143.3 1.5 collective-permute-done.4
  144.9 0.6 fusion.15
  145.8 0.2 fusion.43
  146.0 1.9 collective-permute-start.7
  147.9 6.1 %collective-permute-start.6 = (f32[8,1,32,128]{3,2,1,0:T(8,128)S(1)}, f32[8,1,32,128]{3,2,1,0:T(8,128)S(1)}, u32[]{:S(2)}, u32[]{:S(2)}) collective-permute-start(f32[8,1,32,128]{3,2,1,0:T(8,128)S(1)} %get-tuple-element.13), channel_id=1, source_target_pairs={{32,0},{64,32},{96,64},{128,96},{160,128},{192,160},{224,192},{256... | collective-permute-start | bytes 393224 | tf_op jit(solution)/shard_map/ppermute | solution.py:21
  154.3 1.5 collective-permute-done.6
  155.8 1.4 fusion.8
  157.3 13.0 %scatter_custom_fusion.1 = f32[16384,8]{1,0:T(8,128)} fusion(s32[1024]{0:T(1024)S(1)} %copy-done.10, f32[]{:T(128)} %constant.6.clone.1, f32[1024]{0:T(1024)S(1)} %copy-done.7, f32[768,8]{1,0:T(8,128)S(1)} %copy-done.6, s32[1024]{0:T(1024)S(1)} %fusion.39), kind=kCustom, calls=%fused_computation.4 | custom fusion | flops 16384 | bytes 925700 | tf_op jit(solution)/shard_map/scatter-add | solution.py:47
  170.3 5.1 %copy.9 = f32[8,4,32,128]{3,2,1,0:T(8,128)S(1)} copy(f32[8,4,32,128]{0,3,2,1:T(8,128)} %bitcast.7) | data formatting | bytes 1048576 | tf_op jit(solution)/shard_map/reshape | solution.py:49
  175.5 1.1 fusion.58
  176.7 295.0 %all-reduce.2.cloned.1.call-done = f32[8,4,32,128]{3,2,1,0:T(8,128)} async-done(((f32[8,4,32,128]{3,2,1,0:T(8,128)}), f32[8,4,32,128]{3,2,1,0:T(8,128)}) %all-reduce.2.cloned.1.call-update) | async-done | bytes 524304 | tf_op jit(solution)/shard_map/psum | solution.py:60
  471.6 2.7 fusion.31
  (43 shorter events, 1.2 us)
Async XLA Ops:
  6.5 35.1 %copy-start = (f32[8,4,32,128]{3,2,1,0:T(8,128)S(1)}, f32[8,4,32,128]{3,2,1,0:T(8,128)}, u32[]{:S(2)}) copy-start(f32[8,4,32,128]{3,2,1,0:T(8,128)} %param.6) | copy-start | bytes 1572868
  6.5 465.1 %all-reduce.2.cloned.1.call-start = ((), (), s32[]{:S(2)}) async-start(), calls=%async_computation | async-start | bytes 1048576 | tf_op jit(solution)/shard_map/psum | solution.py:60
  8.3 168.4 %collective-permute-start.1 = (f32[8,1,32,128]{3,2,1,0:T(8,128)}, f32[8,1,32,128]{3,2,1,0:T(8,128)S(1)}, u32[]{:S(2)}, u32[]{:S(2)}) collective-permute-start(f32[8,1,32,128]{3,2,1,0:T(8,128)} %get-tuple-element.44), channel_id=1, source_target_pairs={{0,32},{32,64},{64,96},{96,128},{128,160},{160,192},{192,224},{224... | collective-permute-start | bytes 393224 | tf_op jit(solution)/shard_map/ppermute | solution.py:20
  13.1 163.5 %collective-permute-start = (f32[8,1,32,128]{3,2,1,0:T(8,128)}, f32[8,1,32,128]{3,2,1,0:T(8,128)S(1)}, u32[]{:S(2)}, u32[]{:S(2)}) collective-permute-start(f32[8,1,32,128]{3,2,1,0:T(8,128)} %get-tuple-element.43), channel_id=1, source_target_pairs={{32,0},{64,32},{96,64},{128,96},{160,128},{192,160},{224,192},{256... | collective-permute-start | bytes 393224 | tf_op jit(solution)/shard_map/ppermute | solution.py:21
  28.2 104.9 %collective-permute-start.3 = (f32[8,1,32,128]{3,2,1,0:T(8,128)}, f32[8,1,32,128]{3,2,1,0:T(8,128)}, u32[]{:S(2)}, u32[]{:S(2)}) collective-permute-start(f32[8,1,32,128]{3,2,1,0:T(8,128)} %get-tuple-element.34), channel_id=1, source_target_pairs={{0,32},{32,64},{64,96},{96,128},{128,160},{160,192},{192,224},{224... | collective-permute-start | bytes 393224 | tf_op jit(solution)/shard_map/ppermute | solution.py:20
  30.1 15.3 %copy-start.10 = (s32[1024]{0:T(1024)S(1)}, s32[1024]{0:T(1024)}, u32[]{:S(2)}) copy-start(s32[1024]{0:T(1024)} %param.8) | copy-start | bytes 12292
  30.1 15.3 %copy-start.7 = (f32[1024]{0:T(1024)S(1)}, f32[1024]{0:T(1024)}, u32[]{:S(2)}) copy-start(f32[1024]{0:T(1024)} %param.10) | copy-start | bytes 12292
  30.1 15.3 %copy-start.9 = (s32[1024]{0:T(1024)S(1)}, s32[1024]{0:T(1024)}, u32[]{:S(2)}) copy-start(s32[1024]{0:T(1024)} %param.9) | copy-start | bytes 12292
  30.1 102.9 %collective-permute-start.2 = (f32[8,1,32,128]{3,2,1,0:T(8,128)}, f32[8,1,32,128]{3,2,1,0:T(8,128)}, u32[]{:S(2)}, u32[]{:S(2)}) collective-permute-start(f32[8,1,32,128]{3,2,1,0:T(8,128)} %get-tuple-element.33), channel_id=1, source_target_pairs={{32,0},{64,32},{96,64},{128,96},{160,128},{192,160},{224,192},{256... | collective-permute-start | bytes 393224 | tf_op jit(solution)/shard_map/ppermute | solution.py:21
  43.9 87.2 %copy-start.8 = (f32[768]{0:T(1024)S(1)}, f32[768]{0:T(1024)}, u32[]{:S(2)}) copy-start(f32[768]{0:T(1024)} %param.11) | copy-start | bytes 9220
  43.9 89.1 %copy-start.5 = (f32[1,4,32,128]{3,2,1,0:T(8,128)S(1)}, f32[1,4,32,128]{3,2,1,0:T(8,128)}, u32[]{:S(2)}) copy-start(f32[1,4,32,128]{3,2,1,0:T(8,128)} %param.7) | copy-start | bytes 196612
  135.5 7.8 %collective-permute-start.5 = (f32[8,1,32,128]{3,2,1,0:T(8,128)S(1)}, f32[8,1,32,128]{3,2,1,0:T(8,128)S(1)}, u32[]{:S(2)}, u32[]{:S(2)}) collective-permute-start(f32[8,1,32,128]{3,2,1,0:T(8,128)S(1)} %get-tuple-element.24), channel_id=1, source_target_pairs={{0,32},{32,64},{64,96},{96,128},{128,160},{160,192},{192,224},{224... | collective-permute-start | bytes 393224 | tf_op jit(solution)/shard_map/ppermute | solution.py:20
  137.6 7.2 %collective-permute-start.4 = (f32[8,1,32,128]{3,2,1,0:T(8,128)S(1)}, f32[8,1,32,128]{3,2,1,0:T(8,128)S(1)}, u32[]{:S(2)}, u32[]{:S(2)}) collective-permute-start(f32[8,1,32,128]{3,2,1,0:T(8,128)S(1)} %get-tuple-element.23), channel_id=1, source_target_pairs={{32,0},{64,32},{96,64},{128,96},{160,128},{192,160},{224,192},{256... | collective-permute-start | bytes 393224 | tf_op jit(solution)/shard_map/ppermute | solution.py:21
  144.8 12.4 %copy-start.6 = (f32[768,8]{1,0:T(8,128)S(1)}, f32[768,8]{1,0:T(8,128)}, u32[]{:S(2)}) copy-start(f32[768,8]{1,0:T(8,128)} %broadcast_multiply_fusion) | copy-start | bytes 73732
  146.0 8.2 %collective-permute-start.7 = (f32[8,1,32,128]{3,2,1,0:T(8,128)S(1)}, f32[8,1,32,128]{3,2,1,0:T(8,128)S(1)}, u32[]{:S(2)}, u32[]{:S(2)}) collective-permute-start(f32[8,1,32,128]{3,2,1,0:T(8,128)S(1)} %get-tuple-element.14), channel_id=1, source_target_pairs={{0,32},{32,64},{64,96},{96,128},{128,160},{160,192},{192,224},{224... | collective-permute-start | bytes 393224 | tf_op jit(solution)/shard_map/ppermute | solution.py:20
  147.9 7.8 %collective-permute-start.6 = (f32[8,1,32,128]{3,2,1,0:T(8,128)S(1)}, f32[8,1,32,128]{3,2,1,0:T(8,128)S(1)}, u32[]{:S(2)}, u32[]{:S(2)}) collective-permute-start(f32[8,1,32,128]{3,2,1,0:T(8,128)S(1)} %get-tuple-element.13), channel_id=1, source_target_pairs={{32,0},{64,32},{96,64},{128,96},{160,128},{192,160},{224,192},{256... | collective-permute-start | bytes 393224 | tf_op jit(solution)/shard_map/ppermute | solution.py:21
  157.3 314.4 %copy-start.1 = (f32[8,4,31,128]{3,2,1,0:T(8,128)S(1)}, f32[8,4,31,128]{3,2,1,0:T(8,128)}, u32[]{:S(2)}) copy-start(f32[8,4,31,128]{3,2,1,0:T(8,128)} %get-tuple-element.41) | copy-start | bytes 1523716
  157.3 314.4 %copy-start.2 = (f32[8,4,31,128]{3,2,1,0:T(8,128)S(1)}, f32[8,4,31,128]{3,2,1,0:T(8,128)}, u32[]{:S(2)}) copy-start(f32[8,4,31,128]{3,2,1,0:T(8,128)} %get-tuple-element.42) | copy-start | bytes 1523716
  157.3 314.3 %copy-start.3 = (f32[8,4,32,1]{3,2,1,0:T(8,128)S(1)}, f32[8,4,32,1]{3,2,1,0:T(8,128)}, u32[]{:S(2)}) copy-start(f32[8,4,32,1]{3,2,1,0:T(8,128)} %get-tuple-element.35) | copy-start | bytes 12292
  157.3 314.3 %copy-start.4 = (f32[8,4,32,1]{3,2,1,0:T(8,128)S(1)}, f32[8,4,32,1]{3,2,1,0:T(8,128)}, u32[]{:S(2)}) copy-start(f32[8,4,32,1]{3,2,1,0:T(8,128)} %get-tuple-element.36) | copy-start | bytes 12292
Sparse Core Ops, SparseCore 0:
  157.4 314.2 all-reduce.1
where the time goes:
time: 482 us; the launch traced here: 481 us
  waiting for transfers between devices  299 us (62%)
  blocking collectives  72.6 us (15%)
  starting transfers between devices  41 us (9%)
  other arithmetic  35.8 us (7%)
  local copies, waits for them, and re-layouts  19.6 us (4%)
  between operations  13.7 us (3%)
    psum x1, waiting for transfers between devices, per_device(): summed = lax.psum(partial_value, 'band')  295 us
    psum x1, blocking collectives, per_device(): coefficient = lax.psum(coefficient, 'grid')  72.6 us
    ppermute x4, starting transfers between devices, extended(): after = lax.ppermute(initial, axis, down)  30.2 us
    scatter-add x1, other arithmetic, per_device(): jax.ops.segment_sum((values * entry_value[None, :]).T, entry_proj, num_se...  13 us
    scatter-add x1, other arithmetic, per_device(): jax.ops.segment_sum(contrib, entry_cell, num_segments=flattened.shape[1])  13 us
    ppermute x4, starting transfers between devices, extended(): before = lax.ppermute(last, axis, up)  10.7 us
  transfers between devices with their start and end apart: 9, of which 5 were waited for; matrix products, arithmetic and copies ran while one was open for 11% of the time, Pallas kernels for 0%

commit v1 on v0

v1 whole, which is shorter than its diff:
```python
import functools

import jax
import jax.numpy as jnp
from jax import lax
from jax.experimental import pallas as pl
from jax.experimental.pallas import tpu as pltpu
from jax.sharding import PartitionSpec as P

screening = 0.5
mixing = 0.25
WIDTH = 3
LANES = 128
CORES = 2
XS, YS = 4, 4
RADIX = ((1, 4), (4, 3), (12, 2))
GROUPS = 4
MESH = pl.DeviceIdType.MESH


def three_parts(x):
    first = x.astype(jnp.bfloat16)
    rest = x - first.astype(jnp.float32)
    second = rest.astype(jnp.bfloat16)
    third = (rest - second.astype(jnp.float32)).astype(jnp.bfloat16)
    return jnp.concatenate([first, second, third], axis=0)


def add_parts(x):
    n = x.shape[0] // 3
    return (x[:n] + x[n : 2 * n]) + x[2 * n :]


def as_row(x):
    return jnp.concatenate([x[i : i + 1] for i in range(x.shape[0])], axis=1)


def roll_sum(u):
    rows, lanes = u.shape[-2:]
    a = u.ndim - 2
    return (pltpu.roll(u, 1, a) + pltpu.roll(u, rows - 1, a)) + (
        pltpu.roll(u, 1, a + 1) + pltpu.roll(u, lanes - 1, a + 1)
    )


def kernel(
    nocc_cores,
    psi, occ, cell, proj, value, gain,
    out,
    psi_ext, occ_ext, cell_v, proj_v, value_v, gain_v,
    hot_lane, hot_proj, part, rs1, red1, rs2, kin, csum, cin, call_, out_v,
    local_sem, send_sem, recv_sem,
):
    planes, rows = psi.shape[1], psi.shape[2]
    orbs = psi.shape[0] // CORES
    per = orbs // GROUPS
    ppx, rpy = planes // XS, rows // YS
    entries = cell.shape[0] * cell.shape[1]
    size = lax.axis_size("grid")
    g, n = lax.axis_index("grid"), lax.axis_index("band")
    c = n % CORES
    y = (n // CORES) % YS
    x = n // (CORES * YS)

    def band(xx, yy, cc):
        return (xx * YS + yy) * CORES + cc

    nxt, prv = (g + 1) % size, (g + size - 1) % size
    sibling = (g, band(x, y, 1 - c))
    xpeers = [(g, band((x + m) % XS, y, c)) for m in range(1, XS)]
    ypeers = [(g, band(x, (y + m) % YS, c)) for m in range(1, YS)]
    gpeers = []
    for stride, count in RADIX:
        digit = (g // stride) % count
        gpeers.append([(g + ((digit + m) % count - digit) * stride, n) for m in range(1, count)])

    def local(i, src, dst):
        copy = pltpu.make_async_copy(src, dst, local_sem.at[i])
        copy.start()
        return copy

    first = c * orbs
    load_entries = [
        local(0, cell, cell_v), local(1, proj, proj_v), local(2, value, value_v), local(3, gain, gain_v),
    ]
    load_psi = local(4, psi.at[pl.ds(first, orbs)], psi_ext.at[:, pl.ds(WIDTH, planes)])
    load_occ = local(5, occ.at[0], occ_ext.at[c, pl.ds(WIDTH, planes)])

    partners = [(nxt, n), (prv, n), sibling] + xpeers + ypeers + [d for ds in gpeers for d in ds]
    barrier = pltpu.get_barrier_semaphore()
    for device in partners:
        pl.semaphore_signal(barrier, inc=1, device_id=device, device_id_type=MESH)
    pl.semaphore_wait(barrier, len(partners))

    copies = []

    def send(src, dst, device):
        i = len(copies)
        copy = pltpu.make_async_remote_copy(
            src_ref=src, dst_ref=dst, send_sem=send_sem.at[i], recv_sem=recv_sem.at[i],
            device_id=device, device_id_type=MESH,
        )
        copy.start()
        copies.append(copy)
        return copy

    low, high = pl.ds(0, WIDTH), pl.ds(WIDTH + planes, WIDTH)
    upper, lower = pl.ds(planes - WIDTH, WIDTH), pl.ds(0, WIDTH)
    occ_up = send(occ.at[0, upper], occ_ext.at[c, low], (nxt, n))
    occ_down = send(occ.at[0, lower], occ_ext.at[c, high], (prv, n))
    occ_core = send(occ.at[0], occ_ext.at[c, pl.ds(WIDTH, planes)], sibling)
    halos = []
    for k in range(GROUPS):
        mine, there = pl.ds(first + k * per, per), pl.ds(k * per, per)
        halos.append([
            send(psi.at[mine, upper], psi_ext.at[there, low], (nxt, n)),
            send(psi.at[mine, lower], psi_ext.at[there, high], (prv, n)),
        ])

    for copy in load_entries:
        copy.wait()
    cells, projs, values = as_row(cell_v[...]), as_row(proj_v[...]), as_row(value_v[...])
    cell_row, cell_lane = cells // LANES, cells % LANES
    proj_row, proj_lane = projs // LANES, projs % LANES
    lanes_at = lax.broadcasted_iota(jnp.int32, (LANES, entries), 0)
    hot_lane[...] = jnp.where(lanes_at == cell_lane, 1.0, 0.0).astype(jnp.bfloat16)
    hot_proj[...] = jnp.where(lanes_at == proj_lane, 1.0, 0.0).astype(jnp.bfloat16)
    eight = lax.broadcasted_iota(jnp.int32, (8, entries), 0)
    proj_mask = eight == proj_row

    load_psi.wait()
    load_occ.wait()
    nn = (((1,), (0,)), ((), ()))
    nt = (((1,), (1,)), ((), ()))

    def dot(a, b, dims):
        return lax.dot_general(a, b, dims, preferred_element_type=jnp.float32)

    cut = orbs // XS if orbs >= XS else 1
    for q in range(cut):
        own = psi_ext[x * cut + q, pl.ds(WIDTH, planes)].reshape(planes * rows, LANES)
        spread = add_parts(dot(three_parts(own), hot_lane[...], nn))
        at = lax.broadcasted_iota(jnp.int32, (planes * rows, entries), 0)
        picked = jnp.sum(jnp.where(at == cell_row, spread, 0.0), axis=0, keepdims=True)
        weight = jnp.where(proj_mask, picked * values, 0.0)
        csum[0, q] = add_parts(dot(three_parts(weight), hot_proj[...], nt))

    def coefficients(stage):
        base = sum(count - 1 for _, count in RADIX[:stage])
        return [send(csum.at[stage], cin.at[base + m], device) for m, device in enumerate(gpeers[stage])]

    def collect(stage, sent):
        base = sum(count - 1 for _, count in RADIX[:stage])
        total = csum[stage]
        for m, copy in enumerate(sent):
            copy.wait_recv()
            total = total + cin[base + m]
        csum[stage + 1] = total

    in_flight = coefficients(0)

    occ_up.wait_recv()
    forward_up = send(occ_ext.at[c, low], occ_ext.at[c, low], sibling)
    occ_down.wait_recv()
    forward_down = send(occ_ext.at[c, high], occ_ext.at[c, high], sibling)

    inverse = 1.0 / (6.0 + screening)

    def exchange(k):
        def one(j, total):
            orbital = occ_ext[j]
            density = psi_ext[k] * orbital
            u = density * inverse
            for s in range(1, WIDTH + 1):
                d = density[s : density.shape[0] - s]
                u = ((u[2:] + u[:-2]) + (roll_sum(u[1:-1]) + d)) * inverse
            return total + orbital[WIDTH : WIDTH + planes] * u

        part[k] = lax.fori_loop(0, CORES, one, jnp.zeros(part.shape[1:], jnp.float32))

    def scatter_x(k):
        sent = []
        for m, device in enumerate(xpeers):
            there = pl.ds(((x + m + 1) % XS) * ppx, ppx)
            sent.append(send(part.at[pl.ds(k * per, per), there], rs1.at[pl.ds(k * per, per), m], device))
        return sent

    def scatter_y(k, sent):
        total = part[pl.ds(k * per, per), pl.ds(x * ppx, ppx)]
        for m, copy in enumerate(sent):
            copy.wait_recv()
            total = total + rs1[pl.ds(k * per, per), m]
        red1[pl.ds(k * per, per)] = total
        later = []
        for m, device in enumerate(ypeers):
            there = pl.ds(pl.multiple_of(((y + m + 1) % YS) * rpy, rpy), rpy)
            later.append(send(red1.at[pl.ds(k * per, per), :, there], rs2.at[pl.ds(k * per, per), m], device))
        return later

    own_rows = pl.ds(pl.multiple_of(y * rpy, rpy), rpy)
    first_sent, second_sent = {}, {}
    for k in range(GROUPS + 1):
        if k < GROUPS:
            for copy in halos[k]:
                copy.wait_recv()
            if k == 0:
                occ_core.wait_recv()
                forward_up.wait_recv()
                forward_down.wait_recv()
            for i in range(k * per, (k + 1) * per):
                exchange(i)
            first_sent[k] = scatter_x(k)
            if k < len(RADIX):
                collect(k, in_flight)
                if k + 1 < len(RADIX):
                    in_flight = coefficients(k + 1)
        if k > 0:
            second_sent[k - 1] = scatter_y(k - 1, first_sent[k - 1])
    for k in range(GROUPS, len(RADIX)):
        collect(k, in_flight)
        if k + 1 < len(RADIX):
            in_flight = coefficients(k + 1)

    gains = jnp.concatenate([gain_v[...], jnp.zeros((8 - gain_v.shape[0], LANES), jnp.float32)], axis=0)
    for q in range(cut):
        call_[x * cut + q] = csum[len(RADIX), q] * gains
    mine = pl.ds(x * cut, cut)
    in_flight = [send(call_.at[mine], call_.at[mine], device) for device in xpeers]

    for k in range(orbs):
        for q in range(ppx):
            at = WIDTH + x * ppx + q
            centre = psi_ext[k, at]
            around = (psi_ext[k, at + 1] + psi_ext[k, at - 1]) + roll_sum(centre)
            kin[k, q] = -0.5 * (around - 6.0 * centre)

    for copy in in_flight:
        copy.wait_recv()
    found = add_parts(dot(three_parts(call_[...].reshape(orbs * 8, LANES)), hot_proj[...], nn))
    target = []
    for k in range(orbs):
        picked = jnp.sum(jnp.where(proj_mask, found[k * 8 : (k + 1) * 8], 0.0), axis=0, keepdims=True)
        target.append(picked * values)
    at = lax.broadcasted_iota(jnp.int32, (rpy, entries), 0)
    nonlocal_terms = []
    for q in range(ppx):
        row_mask = at + ((x * ppx + q) * rows + y * rpy) == cell_row
        spread = jnp.concatenate([jnp.where(row_mask, t, 0.0) for t in target], axis=0)
        nonlocal_terms.append(add_parts(dot(three_parts(spread), hot_lane[...], nt)).reshape(orbs, 1, rpy, LANES))
    nonlocal_term = jnp.concatenate(nonlocal_terms, axis=1)

    total = red1[:, :, own_rows]
    for k in range(GROUPS):
        for copy in second_sent[k]:
            copy.wait_recv()
    for m in range(YS - 1):
        total = total + rs2[:, m]
    own_orbs, own_planes = pl.ds(first, orbs), pl.ds(x * ppx, ppx)
    out_v[own_orbs, own_planes, own_rows] = (kin[:, :, own_rows] + nonlocal_term) - mixing * total

    block = out_v.at[own_orbs, own_planes, own_rows]
    in_flight = [send(block, block, device) for device in ypeers]
    for copy in in_flight:
        copy.wait_recv()
    block = out_v.at[own_orbs, own_planes]
    in_flight = [send(block, block, device) for device in xpeers]
    to_core = [send(block, out.at[own_orbs, own_planes], sibling)]
    stores = [local(6, block, out.at[own_orbs, own_planes])]
    for m, copy in enumerate(in_flight):
        copy.wait_recv()
        at = pl.ds(((x + XS - 1 - m) % XS) * ppx, ppx)
        block = out_v.at[own_orbs, at]
        to_core.append(send(block, out.at[own_orbs, at], sibling))
        stores.append(local(7 + m, block, out.at[own_orbs, at]))
    for copy in to_core:
        copy.wait_recv()
    for copy in stores:
        copy.wait()
    for copy in copies:
        copy.wait_send()


def n_copies():
    coefficient = sum(count - 1 for _, count in RADIX) + XS - 1
    return 3 + 2 + GROUPS * (2 + XS - 1 + YS - 1) + coefficient + (YS - 1) + (XS - 1) + XS


def per_device(psi_block, occupied, entry_cell, entry_proj, entry_value, proj_gain):
    nblock, planes, rows, lanes = psi_block.shape
    orbs = nblock // CORES
    entries = entry_cell.shape[0]
    f32 = jnp.float32
    table = (entries // LANES, LANES)
    ext = planes + 2 * WIDTH
    ppx, rpy = planes // XS, rows // YS
    cut = orbs // XS if orbs >= XS else 1
    gains = proj_gain.reshape(-1, LANES)
    total = n_copies()
    any_ = pl.BlockSpec(memory_space=pl.ANY)
    return pl.pallas_call(
        functools.partial(kernel, CORES),
        out_shape=jax.ShapeDtypeStruct(psi_block.shape, f32),
        in_specs=[pl.BlockSpec(memory_space=pltpu.HBM)] * 6,
        out_specs=any_,
        scratch_shapes=[
            pltpu.VMEM((orbs, ext, rows, lanes), f32),
            pltpu.VMEM((CORES, ext, rows, lanes), f32),
            pltpu.VMEM(table, jnp.int32),
            pltpu.VMEM(table, jnp.int32),
            pltpu.VMEM(table, f32),
            pltpu.VMEM(gains.shape, f32),
            pltpu.VMEM((LANES, entries), jnp.bfloat16),
            pltpu.VMEM((LANES, entries), jnp.bfloat16),
            pltpu.VMEM((orbs, planes, rows, lanes), f32),
            pltpu.VMEM((orbs, XS - 1, ppx, rows, lanes), f32),
            pltpu.VMEM((orbs, ppx, rows, lanes), f32),
            pltpu.VMEM((orbs, YS - 1, ppx, rpy, lanes), f32),
            pltpu.VMEM((orbs, ppx, rows, lanes), f32),
            pltpu.VMEM((len(RADIX) + 1, cut, 8, lanes), f32),
            pltpu.VMEM((sum(count - 1 for _, count in RADIX), cut, 8, lanes), f32),
            pltpu.VMEM((orbs, 8, lanes), f32),
            pltpu.VMEM(psi_block.shape, f32),
            pltpu.SemaphoreType.DMA((7 + XS - 1,)),
            pltpu.SemaphoreType.DMA((total,)),
            pltpu.SemaphoreType.DMA((total,)),
        ],
        compiler_params=pltpu.CompilerParams(
            collective_id=0, has_side_effects=True, vmem_limit_bytes=60 * 1024 * 1024
        ),
        cost_estimate=pl.CostEstimate(flops=20_000_000, bytes_accessed=2_000_000, transcendentals=0),
    )(
        psi_block, occupied, entry_cell.reshape(table), entry_proj.reshape(table),
        entry_value.reshape(table), gains,
    )


def solution(mesh):
    in_specs = (
        P(None, "grid", None, None),
        P("band", "grid", None, None),
        P("grid"),
        P("grid"),
        P("grid"),
        P(),
    )
    out_specs = P(None, "grid", None, None)
    return jax.shard_map(
        per_device, mesh=mesh, in_specs=in_specs, out_specs=out_specs, check_vma=False
    )
```

time: 482 us -> 57.7 us (0.12)
  waiting for transfers between devices: 299 us -> 0 us
  blocking collectives: 72.6 us -> 0 us
  Pallas kernels: 0 us -> 55.6 us
  starting transfers between devices: 41 us -> 0 us
  other arithmetic: 35.8 us -> 0 us
  local copies, waits for them, and re-layouts: 19.6 us -> 1.87 us
  between operations: 13.7 us -> 0.01 us
    psum x1 -> x0, waiting for transfers between devices: 295 us -> none  [per_device(): summed = lax.psum(partial_value, 'band')]
    psum x1 -> x0, blocking collectives: 72.6 us -> none  [per_device(): coefficient = lax.psum(coefficient, 'grid')]
    pallas_call x0 -> x1, Pallas kernels: none -> 55.6 us  [per_device(): pl.pallas_call(functools.partial(kernel, CORES), out_shape=jax.ShapeDtype...]
    ppermute x8 -> x0, starting transfers between devices: 41 us -> none  [the longest x4 30.2 us: extended(): after = lax.ppermute(initial, axis, down)]
    scatter-add x2 -> x0, other arithmetic: 26.1 us -> none  [the longest x1 13 us: per_device(): jax.ops.segment_sum((values * entry_value[None, :]).T, entry_proj, num_se...]
    slice x20 -> x0, local copies, waits for them, and re-layouts: 8.48 us -> none  [the longest x8 4.47 us: relax_once(): summed = summed + jnp.roll(center, -1, 3) + jnp.roll(center, 1, 3)]
    reshape x1 -> x0, local copies, waits for them, and re-layouts: 5.14 us -> none  [per_device(): nonlocal_term = jax.ops.segment_sum(contrib, entry_cell, num_segments=fla...]
  transfers between devices with their start and end apart: 9 -> 0, of which waited for: 5 -> 0; matrix products, arithmetic and copies ran while one was open for 11% -> 0% of each run, Pallas kernels for 0% -> 0%
where the time goes in v1:
time: 57.7 us; the launch traced here: 57.5 us
  Pallas kernels  55.6 us (96%)
  local copies, waits for them, and re-layouts  1.87 us (3%)
    pallas_call x1, Pallas kernels, per_device(): pl.pallas_call(functools.partial(kernel, CORES), out_shape=jax.ShapeDtype...  55.6 us
    unnamed x1, local copies, waits for them, and re-layouts  1.87 us

profile of v1, /device:TPU:1, one launch (start us, length us, event | category | flops | bytes accessed | tf_op | source)
XLA Modules:
  0.0 57.5 jit_solution(7629474742850572910)
XLA Ops:
  0.0 55.6 %shard_map.64 = f32[8,4,32,128]{3,2,1,0:T(8,128)} custom-call(f32[8,4,32,128]{3,2,1,0:T(8,128)} %psi.1, f32[1,4,32,128]{3,2,1,0:T(8,128)} %occ.1, s32[8,128]{1,0:T(8,128)} %bitcast.4, s32[8,128]{1,0:T(8,128)} %bitcast.5, f32[8,128]{1,0:T(8,128)} %bitcast.6, f32[6,128]{1,0:T(8,128)} %bitcast.7), custom_call_target="tpu_custom_call" | custom-call | flops 20000000 | bytes 2000000 | tf_op jit(solution)/shard_map/pallas_call | solution.py:300
  55.6 1.9 %copy.8 = f32[8,4,32,128]{3,2,1,0:T(8,128)} copy(f32[8,4,32,128]{3,2,1,0:T(8,128)} %shard_map.64) | data formatting | bytes 1048576

commit v2 on v1

v2 whole, which is shorter than its diff:
```python
import functools

import jax
import jax.numpy as jnp
from jax import lax
from jax.experimental import pallas as pl
from jax.experimental.pallas import tpu as pltpu
from jax.sharding import PartitionSpec as P

screening = 0.5
mixing = 0.25
WIDTH = 3
LANES = 128
CORES = 2
XS, YS = 4, 4
STEPS = ((1, 2), (2, 2), (0, 2), (4, 3))
YLO = 2
DIRECT = 1
GROUPS = 4
FIRST = 2
MESH = pl.DeviceIdType.MESH


def three_parts(x):
    first = x.astype(jnp.bfloat16)
    rest = x - first.astype(jnp.float32)
    second = rest.astype(jnp.bfloat16)
    third = (rest - second.astype(jnp.float32)).astype(jnp.bfloat16)
    return jnp.concatenate([first, second, third], axis=0)


def add_parts(x):
    n = x.shape[0] // 3
    return (x[:n] + x[n : 2 * n]) + x[2 * n :]


def as_row(x):
    return jnp.concatenate([x[i : i + 1] for i in range(x.shape[0])], axis=1)


def roll_sum(u):
    rows, lanes = u.shape[-2:]
    a = u.ndim - 2
    return (pltpu.roll(u, 1, a) + pltpu.roll(u, rows - 1, a)) + (
        pltpu.roll(u, 1, a + 1) + pltpu.roll(u, lanes - 1, a + 1)
    )


def kernel(
    nocc_cores,
    psi, occ, cell, proj, value, gain,
    out,
    psi_ext, occ_ext, cell_v, proj_v, value_v, gain_v,
    hot_lane, hot_proj, part, rs1, red1, rs2, kin, csum, cin, call_,
    local_sem, send_sem, recv_sem, step_sem,
):
    planes, rows = psi.shape[1], psi.shape[2]
    orbs = psi.shape[0] // CORES
    per = orbs // GROUPS
    ppx = planes // XS
    entries = cell.shape[0] * cell.shape[1]
    size = lax.axis_size("grid")
    ring = size // YLO
    g, n = lax.axis_index("grid"), lax.axis_index("band")
    c = lax.rem(n, CORES)
    y = lax.rem(lax.div(n, CORES), YS)
    x = lax.div(n, CORES * YS)

    def wrap(i, length):
        return jnp.where(i >= length, i - length, i)

    def band(xx, yy, cc):
        return (xx * YS + yy) * CORES + cc

    nxt, prv = (wrap(g + 1, size), n), (wrap(g + size - 1, size), n)
    sibling = (g, band(x, y, 1 - c))
    xpeers = [(g, band(wrap(x + m, XS), y, c)) for m in range(1, XS)]
    ypeers = [(g, band(x, wrap(y + m, YS), c)) for m in range(1, YS)]
    z = g
    for i in range(1, YLO):
        z = jnp.where(g >= i * ring, g - i * ring, z)
    turn = g - z

    def along(m):
        return (turn + wrap(z + m % ring, ring), n)

    across = [(wrap(g + m * ring, size), n) for m in range(1, YLO)]

    partners = [nxt, prv, sibling, along(1), along(-1)] + across
    partners += [peers[i] for peers in (xpeers, ypeers) if peers for i in (0, -1)]
    barrier = pltpu.get_barrier_semaphore()

    def signal(semaphore, device):
        pl.semaphore_signal(semaphore, inc=1, device_id=device, device_id_type=MESH)

    for device in partners:
        signal(barrier, device)

    def local(i, src, dst):
        copy = pltpu.make_async_copy(src, dst, local_sem.at[i])
        copy.start()
        return copy

    first = c * orbs
    load_entries = [
        local(0, cell, cell_v), local(1, proj, proj_v), local(2, value, value_v), local(3, gain, gain_v),
    ]
    load_psi = local(4, psi.at[pl.ds(first, orbs)], psi_ext.at[:, pl.ds(WIDTH, planes)])
    load_occ = local(5, occ.at[0], occ_ext.at[c, pl.ds(WIDTH, planes)])

    for copy in load_entries:
        copy.wait()
    cells, projs, values = as_row(cell_v[...]), as_row(proj_v[...]), as_row(value_v[...])
    cell_row, cell_lane = cells // LANES, cells % LANES
    proj_row, proj_lane = projs // LANES, projs % LANES
    lanes_at = lax.broadcasted_iota(jnp.int32, (LANES, entries), 0)
    hot_lane[...] = jnp.where(lanes_at == cell_lane, 1.0, 0.0).astype(jnp.bfloat16)
    hot_proj[...] = jnp.where(lanes_at == proj_lane, 1.0, 0.0).astype(jnp.bfloat16)
    eight = lax.broadcasted_iota(jnp.int32, (8, entries), 0)
    proj_mask = eight == proj_row

    load_psi.wait()
    load_occ.wait()
    nn = (((1,), (0,)), ((), ()))
    nt = (((1,), (1,)), ((), ()))

    def dot(a, b, dims):
        return lax.dot_general(a, b, dims, preferred_element_type=jnp.float32)

    cut = orbs // XS if orbs >= XS else 1
    for q in range(cut):
        own = psi_ext[x * cut + q, pl.ds(WIDTH, planes)].reshape(planes * rows, LANES)
        spread = add_parts(dot(three_parts(own), hot_lane[...], nn))
        at = lax.broadcasted_iota(jnp.int32, (planes * rows, entries), 0)
        picked = jnp.sum(jnp.where(at == cell_row, spread, 0.0), axis=0, keepdims=True)
        weight = jnp.where(proj_mask, picked * values, 0.0)
        csum[0, q] = add_parts(dot(three_parts(weight), hot_proj[...], nt))

    pl.semaphore_wait(barrier, len(partners))

    copies = []

    def send(src, dst, device):
        i = len(copies)
        copy = pltpu.make_async_remote_copy(
            src_ref=src, dst_ref=dst, send_sem=send_sem.at[i], recv_sem=recv_sem.at[i],
            device_id=device, device_id_type=MESH,
        )
        copy.start()
        copies.append(copy)
        return copy

    low, high = pl.ds(0, WIDTH), pl.ds(WIDTH + planes, WIDTH)
    upper, lower = pl.ds(planes, WIDTH), pl.ds(WIDTH, WIDTH)

    def halo(k):
        there = pl.ds(k * per, per)
        return [
            send(psi_ext.at[there, upper], psi_ext.at[there, low], nxt),
            send(psi_ext.at[there, lower], psi_ext.at[there, high], prv),
        ]

    word = [i for i, (distance, terms) in enumerate(STEPS[:-1]) if distance and terms == 2]

    def coefficients(stage):
        base = sum(terms - 1 for _, terms in STEPS[:stage])
        distance, terms = STEPS[stage]
        if not distance:
            devices = across
        elif terms == 2:
            devices = [along(-distance)]
            if stage in word:
                signal(step_sem.at[1 + stage], along(distance))
        else:
            devices = [along(distance), along(-distance)]
        return [send(csum.at[stage], cin.at[base + m], device) for m, device in enumerate(devices)]

    def collect(stage, sent):
        base = sum(terms - 1 for _, terms in STEPS[:stage])
        total = csum[stage]
        for m, copy in enumerate(sent):
            copy.wait_recv()
            total = total + cin[base + m]
        csum[stage + 1] = total
        if stage in word:
            pl.semaphore_wait(step_sem.at[1 + stage], 1)

    stages = len(STEPS)
    steps = [coefficients(0)]

    def next_step():
        stage = len(steps) - 1
        if stage >= stages:
            return
        collect(stage, steps[stage])
        steps.append(coefficients(stage + 1) if stage + 1 < stages else None)

    occ_halo = [
        send(occ_ext.at[c, upper], occ_ext.at[c, low], nxt), send(occ_ext.at[c, lower], occ_ext.at[c, high], prv),
    ]
    centre = occ_ext.at[c, pl.ds(WIDTH, planes)]
    occ_core = send(centre, centre, sibling)
    halos = [halo(k) for k in range(FIRST)]
    greeted = [peers[-1] for peers in (xpeers, ypeers) if peers]
    for device in greeted:
        signal(step_sem.at[0], device)
    next_step()
    halos += [halo(k) for k in range(FIRST, GROUPS)]
    for copy, part_ in zip(occ_halo, (low, high)):
        copy.wait_recv()
        block = occ_ext.at[c, part_]
        send(block, block, sibling)
    forwards = copies[-2:]

    inverse = 1.0 / (6.0 + screening)

    def exchange(k):
        def one(j, total):
            orbital = occ_ext[j]
            density = psi_ext[k] * orbital
            u = density * inverse
            for s in range(1, WIDTH + 1):
                d = density[s : density.shape[0] - s]
                u = ((u[2:] + u[:-2]) + (roll_sum(u[1:-1]) + d)) * inverse
            return total + orbital[WIDTH : WIDTH + planes] * u

        part[k] = lax.fori_loop(0, CORES, one, jnp.zeros(part.shape[1:], jnp.float32))

    def scatter_x(k):
        sent = []
        for m, device in enumerate(xpeers):
            there = pl.ds(((x + m + 1) % XS) * ppx, ppx)
            sent.append(send(part.at[pl.ds(k * per, per), there], rs1.at[pl.ds(k * per, per), m], device))
        return sent

    def sum_x(k, sent):
        own = pl.ds(k * per, per)
        total = part[own, pl.ds(x * ppx, ppx)]
        for m, copy in enumerate(sent):
            copy.wait_recv()
            total = total + rs1[own, m]
        red1[own] = total
        return [send(red1.at[own], rs2.at[own, m], device) for m, device in enumerate(ypeers)]

    def share_coefficients():
        while len(steps) <= stages:
            next_step()
        gains = jnp.concatenate([gain_v[...], jnp.zeros((8 - gain_v.shape[0], LANES), jnp.float32)], axis=0)
        for q in range(cut):
            call_[x * cut + q] = csum[stages, q] * gains
        mine = pl.ds(x * cut, cut)
        return [send(call_.at[mine], call_.at[mine], device) for device in xpeers]

    first_sent, second_sent = [], []
    for k in range(GROUPS):
        for copy in halos[k]:
            copy.wait_recv()
        if k == 0:
            for copy in [occ_core] + forwards:
                copy.wait_recv()
            pl.semaphore_wait(step_sem.at[0], len(greeted))
        for i in range(k * per, (k + 1) * per):
            exchange(i)
        first_sent.append(scatter_x(k))
        if k == 1:
            next_step()
    next_step()
    for k in range(GROUPS):
        second_sent.append(sum_x(k, first_sent[k]))
    share = share_coefficients()

    for k in range(orbs):
        for q in range(ppx):
            at = WIDTH + x * ppx + q
            centre = psi_ext[k, at]
            around = (psi_ext[k, at + 1] + psi_ext[k, at - 1]) + roll_sum(centre)
            kin[k, q] = -0.5 * (around - 6.0 * centre)

    for copy in share:
        copy.wait_recv()
    found = add_parts(dot(three_parts(call_[...].reshape(orbs * 8, LANES)), hot_proj[...], nn))
    target = []
    for k in range(orbs):
        picked = jnp.sum(jnp.where(proj_mask, found[k * 8 : (k + 1) * 8], 0.0), axis=0, keepdims=True)
        target.append(picked * values)
    at = lax.broadcasted_iota(jnp.int32, (rows, entries), 0)
    for q in range(ppx):
        row_mask = at + (x * ppx + q) * rows == cell_row
        spread = jnp.concatenate([jnp.where(row_mask, t, 0.0) for t in target], axis=0)
        found = add_parts(dot(three_parts(spread), hot_lane[...], nt))
        for k in range(orbs):
            kin[k, q] = kin[k, q] + found[k * rows : (k + 1) * rows]

    xcross = [(g, band(wrap(x + m, XS), y, 1 - c)) for m in range(1, XS)]
    gathered = []
    for k in range(GROUPS):
        own = pl.ds(k * per, per)
        total = red1[own]
        for m, copy in enumerate(second_sent[k]):
            copy.wait_recv()
            total = total + rs2[own, m]
        there = pl.ds(first + k * per, per)
        block = out.at[there, pl.ds(x * ppx, ppx)]
        out[there, pl.ds(x * ppx, ppx)] = kin[own] - mixing * total
        last = k >= GROUPS - DIRECT
        gathered.append([send(block, block, device) for device in xpeers + (xcross if last else []) + [sibling]])
    for k in range(GROUPS - DIRECT):
        for m, copy in enumerate(gathered[k][:-1]):
            copy.wait_recv()
            there = pl.ds(wrap(x + XS - 1 - m, XS) * ppx, ppx)
            block = out.at[pl.ds(first + k * per, per), there]
            gathered[k].append(send(block, block, sibling))
        gathered[k] = gathered[k][XS - 1 :]
    for sent in gathered:
        for copy in sent:
            copy.wait_recv()
    for copy in copies:
        copy.wait_send()


def n_copies():
    coefficient = sum(terms - 1 for _, terms in STEPS) + XS - 1
    return 3 + 2 + GROUPS * (2 + (XS - 1) + (YS - 1) + 2 * XS - 1) + coefficient


def per_device(psi_block, occupied, entry_cell, entry_proj, entry_value, proj_gain):
    nblock, planes, rows, lanes = psi_block.shape
    orbs = nblock // CORES
    entries = entry_cell.shape[0]
    f32 = jnp.float32
    table = (entries // LANES, LANES)
    ext = planes + 2 * WIDTH
    ppx = planes // XS
    cut = orbs // XS if orbs >= XS else 1
    gains = proj_gain.reshape(-1, LANES)
    total = n_copies()
    return pl.pallas_call(
        functools.partial(kernel, CORES),
        out_shape=pltpu.VMEM(psi_block.shape, f32),
        in_specs=[pl.BlockSpec(memory_space=pltpu.HBM)] * 6,
        out_specs=pl.BlockSpec(memory_space=pltpu.VMEM),
        scratch_shapes=[
            pltpu.VMEM((orbs, ext, rows, lanes), f32),
            pltpu.VMEM((CORES, ext, rows, lanes), f32),
            pltpu.VMEM(table, jnp.int32),
            pltpu.VMEM(table, jnp.int32),
            pltpu.VMEM(table, f32),
            pltpu.VMEM(gains.shape, f32),
            pltpu.VMEM((LANES, entries), jnp.bfloat16),
            pltpu.VMEM((LANES, entries), jnp.bfloat16),
            pltpu.VMEM((orbs, planes, rows, lanes), f32),
            pltpu.VMEM((orbs, XS - 1, ppx, rows, lanes), f32),
            pltpu.VMEM((orbs, ppx, rows, lanes), f32),
            pltpu.VMEM((orbs, YS - 1, ppx, rows, lanes), f32),
            pltpu.VMEM((orbs, ppx, rows, lanes), f32),
            pltpu.VMEM((len(STEPS) + 1, cut, 8, lanes), f32),
            pltpu.VMEM((sum(terms - 1 for _, terms in STEPS), cut, 8, lanes), f32),
            pltpu.VMEM((orbs, 8, lanes), f32),
            pltpu.SemaphoreType.DMA((6,)),
            pltpu.SemaphoreType.DMA((total,)),
            pltpu.SemaphoreType.DMA((total,)),
            pltpu.SemaphoreType.REGULAR((1 + len(STEPS),)),
        ],
        compiler_params=pltpu.CompilerParams(
            collective_id=0, has_side_effects=True, vmem_limit_bytes=60 * 1024 * 1024
        ),
        cost_estimate=pl.CostEstimate(flops=20_000_000, bytes_accessed=2_000_000, transcendentals=0),
    )(
        psi_block, occupied, entry_cell.reshape(table), entry_proj.reshape(table),
        entry_value.reshape(table), gains,
    )


def solution(mesh):
    in_specs = (
        P(None, "grid", None, None),
        P("band", "grid", None, None),
        P("grid"),
        P("grid"),
        P("grid"),
        P(),
    )
    out_specs = P(None, "grid", None, None)
    return jax.shard_map(
        per_device, mesh=mesh, in_specs=in_specs, out_specs=out_specs, check_vma=False
    )
```

time: 57.7 us -> 43.3 us (0.75)
  Pallas kernels: 55.6 us -> 42.4 us
  local copies, waits for them, and re-layouts: 1.87 us -> 0.8 us
    pallas_call x1, Pallas kernels: 55.6 us -> 42.4 us  [per_device(): pl.pallas_call(functools.partial(kernel, CORES), out_shape=pltpu.VMEM(psi...]
    unnamed x1, local copies, waits for them, and re-layouts: 1.87 us -> 0.8 us
where the time goes in v2:
time: 43.3 us; the launch traced here: 43.2 us
  Pallas kernels  42.4 us (98%)
  local copies, waits for them, and re-layouts  0.8 us (2%)
    pallas_call x1, Pallas kernels, per_device(): pl.pallas_call(functools.partial(kernel, CORES), out_shape=pltpu.VMEM(psi...  42.4 us

profile of v2, /device:TPU:1, one launch (start us, length us, event | category | flops | bytes accessed | tf_op | source)
XLA Modules:
  0.0 43.2 jit_solution(3601763301038862207)
XLA Ops:
  0.0 42.4 %shard_map.64 = f32[8,4,32,128]{3,2,1,0:T(8,128)S(1)} custom-call(f32[8,4,32,128]{3,2,1,0:T(8,128)} %psi.1, f32[1,4,32,128]{3,2,1,0:T(8,128)} %occ.1, s32[8,128]{1,0:T(8,128)} %bitcast.4, s32[8,128]{1,0:T(8,128)} %bitcast.5, f32[8,128]{1,0:T(8,128)} %bitcast.6, f32[6,128]{1,0:T(8,128)} %bitcast.7), custom_call_target="tpu_custom_call" | custom-call | flops 20000000 | bytes 2000000 | tf_op jit(solution)/shard_map/pallas_call | solution.py:337
  42.4 0.8 %copy.8 = f32[8,4,32,128]{3,2,1,0:T(8,128)} copy(f32[8,4,32,128]{3,2,1,0:T(8,128)S(1)} %shard_map.64) | data formatting | bytes 1048576

commit v3 on v2

--- a/solution.py
+++ b/solution.py
@@ -13,11 +13,11 @@
 LANES = 128
 CORES = 2
 XS, YS = 4, 4
-STEPS = ((1, 2), (2, 2), (0, 2), (4, 3))
+STEPS = ((1, 2, 2), (2, 2, 1), (4, 3, 1))
 YLO = 2
-DIRECT = 1
+DIRECT = 2
 GROUPS = 4
-FIRST = 2
+SHARE = 1
 MESH = pl.DeviceIdType.MESH
 
 
@@ -81,13 +81,14 @@
         z = jnp.where(g >= i * ring, g - i * ring, z)
     turn = g - z
 
-    def along(m):
-        return (turn + wrap(z + m % ring, ring), n)
-
-    across = [(wrap(g + m * ring, size), n) for m in range(1, YLO)]
-
-    partners = [nxt, prv, sibling, along(1), along(-1)] + across
-    partners += [peers[i] for peers in (xpeers, ypeers) if peers for i in (0, -1)]
+    def along(m, over=0):
+        return (wrap(turn + wrap(z + m % ring, ring) + over * ring, size), n)
+
+    partners = [nxt, prv]
+    partners += [along(m, over) for over in range(1, YLO) for m in (-1, 1)]
+    partners += [ypeers[i] for i in (0, -1) if ypeers]
+    partners += [along(1), along(-1)] + [along(0, over) for over in range(1, YLO)]
+    partners += [xpeers[i] for i in (0, -1) if xpeers] + [sibling]
     barrier = pltpu.get_barrier_semaphore()
 
     def signal(semaphore, device):
@@ -160,27 +161,27 @@
             send(psi_ext.at[there, lower], psi_ext.at[there, high], prv),
         ]
 
-    word = [i for i, (distance, terms) in enumerate(STEPS[:-1]) if distance and terms == 2]
+    word = [i for i, (_, terms, _) in enumerate(STEPS[:-1]) if terms == 2]
+    bases = [sum(terms * over - 1 for _, terms, over in STEPS[:i]) for i in range(len(STEPS) + 1)]
+
+    def far_first(peers, one):
+        order = sorted(range(len(peers)), key=lambda m: -min(m + 1, len(peers) - m))
+        sent = {m: one(m, peers[m]) for m in order}
+        return [sent[m] for m in range(len(peers))]
 
     def coefficients(stage):
-        base = sum(terms - 1 for _, terms in STEPS[:stage])
-        distance, terms = STEPS[stage]
-        if not distance:
-            devices = across
-        elif terms == 2:
-            devices = [along(-distance)]
-            if stage in word:
-                signal(step_sem.at[1 + stage], along(distance))
-        else:
-            devices = [along(distance), along(-distance)]
-        return [send(csum.at[stage], cin.at[base + m], device) for m, device in enumerate(devices)]
+        distance, terms, over = STEPS[stage]
+        if stage in word:
+            signal(step_sem.at[1 + stage], along(distance))
+        places = [0, -distance] if terms == 2 else [0, distance, -distance]
+        devices = [along(m, o) for o in range(over) for m in places][1:]
+        return [send(csum.at[stage], cin.at[bases[stage] + m], device) for m, device in enumerate(devices)]
 
     def collect(stage, sent):
-        base = sum(terms - 1 for _, terms in STEPS[:stage])
         total = csum[stage]
         for m, copy in enumerate(sent):
             copy.wait_recv()
-            total = total + cin[base + m]
+            total = total + cin[bases[stage] + m]
         csum[stage + 1] = total
         if stage in word:
             pl.semaphore_wait(step_sem.at[1 + stage], 1)
@@ -200,38 +201,39 @@
     ]
     centre = occ_ext.at[c, pl.ds(WIDTH, planes)]
     occ_core = send(centre, centre, sibling)
-    halos = [halo(k) for k in range(FIRST)]
+    halos = [halo(k) for k in range(GROUPS - 1)]
     greeted = [peers[-1] for peers in (xpeers, ypeers) if peers]
     for device in greeted:
         signal(step_sem.at[0], device)
     next_step()
-    halos += [halo(k) for k in range(FIRST, GROUPS)]
+    halos.append(halo(GROUPS - 1))
     for copy, part_ in zip(occ_halo, (low, high)):
         copy.wait_recv()
         block = occ_ext.at[c, part_]
         send(block, block, sibling)
     forwards = copies[-2:]
 
-    inverse = 1.0 / (6.0 + screening)
+    a = 6.0 + screening
 
     def exchange(k):
-        def one(j, total):
-            orbital = occ_ext[j]
-            density = psi_ext[k] * orbital
-            u = density * inverse
-            for s in range(1, WIDTH + 1):
-                d = density[s : density.shape[0] - s]
-                u = ((u[2:] + u[:-2]) + (roll_sum(u[1:-1]) + d)) * inverse
-            return total + orbital[WIDTH : WIDTH + planes] * u
-
-        part[k] = lax.fori_loop(0, CORES, one, jnp.zeros(part.shape[1:], jnp.float32))
+        orbital = occ_ext[...]
+        density = psi_ext[k][None] * orbital
+
+        def shifted(m):
+            return density[:, WIDTH + m : WIDTH + m + planes]
+
+        d, once, twice, thrice = shifted(0), *(shifted(m) + shifted(-m) for m in range(1, WIDTH + 1))
+        u = (a * d + 3.0 * once) + roll_sum(d)
+        u = (((a * a + 6.0) * d + (2.0 * a) * once) + 3.0 * twice) + roll_sum(u)
+        u = (((a**3 + 2.0 * a) * d + (a * a + 3.0) * once) + (a * twice + thrice)) + roll_sum(u)
+        part[k] = jnp.sum(orbital[:, WIDTH : WIDTH + planes] * u, axis=0) * (1.0 / a**4)
 
     def scatter_x(k):
-        sent = []
-        for m, device in enumerate(xpeers):
-            there = pl.ds(((x + m + 1) % XS) * ppx, ppx)
-            sent.append(send(part.at[pl.ds(k * per, per), there], rs1.at[pl.ds(k * per, per), m], device))
-        return sent
+        def one(m, device):
+            there = pl.ds(wrap(x + m + 1, XS) * ppx, ppx)
+            return send(part.at[pl.ds(k * per, per), there], rs1.at[pl.ds(k * per, per), m], device)
+
+        return far_first(xpeers, one)
 
     def sum_x(k, sent):
         own = pl.ds(k * per, per)
@@ -240,7 +242,7 @@
             copy.wait_recv()
             total = total + rs1[own, m]
         red1[own] = total
-        return [send(red1.at[own], rs2.at[own, m], device) for m, device in enumerate(ypeers)]
+        return far_first(ypeers, lambda m, device: send(red1.at[own], rs2.at[own, m], device))
 
     def share_coefficients():
         while len(steps) <= stages:
@@ -262,12 +264,12 @@
         for i in range(k * per, (k + 1) * per):
             exchange(i)
         first_sent.append(scatter_x(k))
-        if k == 1:
+        if k == 0:
             next_step()
-    next_step()
     for k in range(GROUPS):
         second_sent.append(sum_x(k, first_sent[k]))
-    share = share_coefficients()
+        if k == SHARE:
+            share = share_coefficients()
 
     for k in range(orbs):
         for q in range(ppx):
@@ -303,7 +305,9 @@
         block = out.at[there, pl.ds(x * ppx, ppx)]
         out[there, pl.ds(x * ppx, ppx)] = kin[own] - mixing * total
         last = k >= GROUPS - DIRECT
-        gathered.append([send(block, block, device) for device in xpeers + (xcross if last else []) + [sibling]])
+        sent = far_first(xpeers, lambda m, device: send(block, block, device))
+        sent += far_first(xcross, lambda m, device: send(block, block, device)) if last else []
+        gathered.append(sent + [send(block, block, sibling)])
     for k in range(GROUPS - DIRECT):
         for m, copy in enumerate(gathered[k][:-1]):
             copy.wait_recv()
@@ -319,7 +323,7 @@
 
 
 def n_copies():
-    coefficient = sum(terms - 1 for _, terms in STEPS) + XS - 1
+    coefficient = sum(terms * over - 1 for _, terms, over in STEPS) + XS - 1
     return 3 + 2 + GROUPS * (2 + (XS - 1) + (YS - 1) + 2 * XS - 1) + coefficient
 
 
@@ -354,7 +358,7 @@
             pltpu.VMEM((orbs, YS - 1, ppx, rows, lanes), f32),
             pltpu.VMEM((orbs, ppx, rows, lanes), f32),
             pltpu.VMEM((len(STEPS) + 1, cut, 8, lanes), f32),
-            pltpu.VMEM((sum(terms - 1 for _, terms in STEPS), cut, 8, lanes), f32),
+            pltpu.VMEM((sum(terms * over - 1 for _, terms, over in STEPS), cut, 8, lanes), f32),
             pltpu.VMEM((orbs, 8, lanes), f32),
             pltpu.SemaphoreType.DMA((6,)),
             pltpu.SemaphoreType.DMA((total,)),

time: 43.3 us -> 42 us (0.970)
  Pallas kernels: 42.4 us -> 41.1 us
    pallas_call x1, Pallas kernels: 42.4 us -> 41.1 us  [per_device(): pl.pallas_call(functools.partial(kernel, CORES), out_shape=pltpu.VMEM(psi...]
where the time goes in v3:
time: 42 us; the launch traced here: 41.9 us
  Pallas kernels  41.1 us (98%)
  local copies, waits for them, and re-layouts  0.8 us (2%)
    pallas_call x1, Pallas kernels, per_device(): pl.pallas_call(functools.partial(kernel, CORES), out_shape=pltpu.VMEM(psi...  41.1 us

profile of v3, /device:TPU:1, one launch (start us, length us, event | category | flops | bytes accessed | tf_op | source)
XLA Modules:
  0.0 41.9 jit_solution(17250864816248367393)
XLA Ops:
  0.0 41.1 %shard_map.64 = f32[8,4,32,128]{3,2,1,0:T(8,128)S(1)} custom-call(f32[8,4,32,128]{3,2,1,0:T(8,128)} %psi.1, f32[1,4,32,128]{3,2,1,0:T(8,128)} %occ.1, s32[8,128]{1,0:T(8,128)} %bitcast.4, s32[8,128]{1,0:T(8,128)} %bitcast.5, f32[8,128]{1,0:T(8,128)} %bitcast.6, f32[6,128]{1,0:T(8,128)} %bitcast.7), custom_call_target="tpu_custom_call" | custom-call | flops 20000000 | bytes 2000000 | tf_op jit(solution)/shard_map/pallas_call | solution.py:341
  41.1 0.8 %copy.8 = f32[8,4,32,128]{3,2,1,0:T(8,128)} copy(f32[8,4,32,128]{3,2,1,0:T(8,128)S(1)} %shard_map.64) | data formatting | bytes 1048576

commit v4 on v3

--- a/solution.py
+++ b/solution.py
@@ -200,8 +200,9 @@
         send(occ_ext.at[c, upper], occ_ext.at[c, low], nxt), send(occ_ext.at[c, lower], occ_ext.at[c, high], prv),
     ]
     centre = occ_ext.at[c, pl.ds(WIDTH, planes)]
+    halos = [halo(0)]
     occ_core = send(centre, centre, sibling)
-    halos = [halo(k) for k in range(GROUPS - 1)]
+    halos += [halo(k) for k in range(1, GROUPS - 1)]
     greeted = [peers[-1] for peers in (xpeers, ypeers) if peers]
     for device in greeted:
         signal(step_sem.at[0], device)

time: 42 us -> 42 us (level)
  no operation moved by 1% of the time
where the time goes in v4:
time: 42 us; the launch traced here: 41.9 us
  Pallas kernels  41.1 us (98%)
  local copies, waits for them, and re-layouts  0.8 us (2%)
    pallas_call x1, Pallas kernels, per_device(): pl.pallas_call(functools.partial(kernel, CORES), out_shape=pltpu.VMEM(psi...  41.1 us

profile of v4, /device:TPU:1, one launch (start us, length us, event | category | flops | bytes accessed | tf_op | source)
XLA Modules:
  0.0 41.9 jit_solution(8023905186667105365)
XLA Ops:
  0.0 41.1 %shard_map.64 = f32[8,4,32,128]{3,2,1,0:T(8,128)S(1)} custom-call(f32[8,4,32,128]{3,2,1,0:T(8,128)} %psi.1, f32[1,4,32,128]{3,2,1,0:T(8,128)} %occ.1, s32[8,128]{1,0:T(8,128)} %bitcast.4, s32[8,128]{1,0:T(8,128)} %bitcast.5, f32[8,128]{1,0:T(8,128)} %bitcast.6, f32[6,128]{1,0:T(8,128)} %bitcast.7), custom_call_target="tpu_custom_call" | custom-call | flops 20000000 | bytes 2000000 | tf_op jit(solution)/shard_map/pallas_call | solution.py:342
  41.1 0.8 %copy.8 = f32[8,4,32,128]{3,2,1,0:T(8,128)} copy(f32[8,4,32,128]{3,2,1,0:T(8,128)S(1)} %shard_map.64) | data formatting | bytes 1048576

commit v5 on v4

--- a/solution.py
+++ b/solution.py
@@ -15,9 +15,9 @@
 XS, YS = 4, 4
 STEPS = ((1, 2, 2), (2, 2, 1), (4, 3, 1))
 YLO = 2
-DIRECT = 2
+DIRECT = (2, 3)
 GROUPS = 4
-SHARE = 1
+SHARE = 2
 MESH = pl.DeviceIdType.MESH
 
 
@@ -305,11 +305,11 @@
         there = pl.ds(first + k * per, per)
         block = out.at[there, pl.ds(x * ppx, ppx)]
         out[there, pl.ds(x * ppx, ppx)] = kin[own] - mixing * total
-        last = k >= GROUPS - DIRECT
+        last = k in DIRECT
         sent = far_first(xpeers, lambda m, device: send(block, block, device))
         sent += far_first(xcross, lambda m, device: send(block, block, device)) if last else []
         gathered.append(sent + [send(block, block, sibling)])
-    for k in range(GROUPS - DIRECT):
+    for k in (k for k in range(GROUPS) if k not in DIRECT):
         for m, copy in enumerate(gathered[k][:-1]):
             copy.wait_recv()
             there = pl.ds(wrap(x + XS - 1 - m, XS) * ppx, ppx)

time: 42 us -> 42 us (level)
  no operation moved by 1% of the time
where the time goes in v5:
time: 42 us; the launch traced here: 41.9 us
  Pallas kernels  41.1 us (98%)
  local copies, waits for them, and re-layouts  0.8 us (2%)
    pallas_call x1, Pallas kernels, per_device(): pl.pallas_call(functools.partial(kernel, CORES), out_shape=pltpu.VMEM(psi...  41.1 us

profile of v5, /device:TPU:1, one launch (start us, length us, event | category | flops | bytes accessed | tf_op | source)
XLA Modules:
  0.0 41.9 jit_solution(8018755806142335973)
XLA Ops:
  0.0 41.1 %shard_map.64 = f32[8,4,32,128]{3,2,1,0:T(8,128)S(1)} custom-call(f32[8,4,32,128]{3,2,1,0:T(8,128)} %psi.1, f32[1,4,32,128]{3,2,1,0:T(8,128)} %occ.1, s32[8,128]{1,0:T(8,128)} %bitcast.4, s32[8,128]{1,0:T(8,128)} %bitcast.5, f32[8,128]{1,0:T(8,128)} %bitcast.6, f32[6,128]{1,0:T(8,128)} %bitcast.7), custom_call_target="tpu_custom_call" | custom-call | flops 20000000 | bytes 2000000 | tf_op jit(solution)/shard_map/pallas_call | solution.py:342
  41.1 0.8 %copy.8 = f32[8,4,32,128]{3,2,1,0:T(8,128)} copy(f32[8,4,32,128]{3,2,1,0:T(8,128)S(1)} %shard_map.64) | data formatting | bytes 1048576

commit v6 on v5

--- a/solution.py
+++ b/solution.py
@@ -309,12 +309,14 @@
         sent = far_first(xpeers, lambda m, device: send(block, block, device))
         sent += far_first(xcross, lambda m, device: send(block, block, device)) if last else []
         gathered.append(sent + [send(block, block, sibling)])
-    for k in (k for k in range(GROUPS) if k not in DIRECT):
-        for m, copy in enumerate(gathered[k][:-1]):
-            copy.wait_recv()
-            there = pl.ds(wrap(x + XS - 1 - m, XS) * ppx, ppx)
-            block = out.at[pl.ds(first + k * per, per), there]
-            gathered[k].append(send(block, block, sibling))
+    early = [k for k in range(GROUPS) if k not in DIRECT]
+    for m in range(XS - 1):
+        for k in early:
+            gathered[k][m].wait_recv()
+        there = pl.ds(wrap(x + XS - 1 - m, XS) * ppx, ppx)
+        block = out.at[pl.ds(first, len(early) * per), there]
+        gathered[0].append(send(block, block, sibling))
+    for k in early:
         gathered[k] = gathered[k][XS - 1 :]
     for sent in gathered:
         for copy in sent:

time: 42 us -> 42 us (level)
  no operation moved by 1% of the time
where the time goes in v6:
time: 42 us; the launch traced here: 41.9 us
  Pallas kernels  41.1 us (98%)
  local copies, waits for them, and re-layouts  0.8 us (2%)
    pallas_call x1, Pallas kernels, per_device(): pl.pallas_call(functools.partial(kernel, CORES), out_shape=pltpu.VMEM(psi...  41.1 us

profile of v6, /device:TPU:1, one launch (start us, length us, event | category | flops | bytes accessed | tf_op | source)
XLA Modules:
  0.0 41.9 jit_solution(4974409615692048374)
XLA Ops:
  0.0 41.1 %shard_map.64 = f32[8,4,32,128]{3,2,1,0:T(8,128)S(1)} custom-call(f32[8,4,32,128]{3,2,1,0:T(8,128)} %psi.1, f32[1,4,32,128]{3,2,1,0:T(8,128)} %occ.1, s32[8,128]{1,0:T(8,128)} %bitcast.4, s32[8,128]{1,0:T(8,128)} %bitcast.5, f32[8,128]{1,0:T(8,128)} %bitcast.6, f32[6,128]{1,0:T(8,128)} %bitcast.7), custom_call_target="tpu_custom_call" | custom-call | flops 20000000 | bytes 2000000 | tf_op jit(solution)/shard_map/pallas_call | solution.py:344
  41.1 0.8 %copy.8 = f32[8,4,32,128]{3,2,1,0:T(8,128)} copy(f32[8,4,32,128]{3,2,1,0:T(8,128)S(1)} %shard_map.64) | data formatting | bytes 1048576
